TPU v7x, 256 devices: a whole 4x4x8 slice. The times are simulated.
256 devices in a mesh: tr: 16 (over x_hi, z), tc: 16 (over y, x_lo, core).
Axes of the slice: x: 4 (x_hi: 2, x_lo: 2; x = x_hi * 2 + x_lo), y: 4, z: 8, core: 2. Of those that a mesh axis runs over, the one named last changes fastest.
Arguments:
- diag_block: bfloat16 [16, 16, 1024, 1024], P('tr', 'tc'), as said below
- coupling: bfloat16 [16, 16, 1024, 1024], P('tr', 'tc'), may hold values from -0.09375 to 0.09375
- precond: float32 [16, 16, 1024, 1024], P('tr', 'tc'), as said below
- rhs: float32 [16, 16, 1024, 128], P('tr', 'tc')
- slot_time: int32 [16, 16], P('tr', 'tc'), may hold values from 0 to 255, as said below
Outputs:
- solution: float32 [16, 16, 1024, 128], P('tr', 'tc')
- residual_norm: float32 [128], replicated
Inputs may be any that keep to these rules, and one draw needn't show every extreme that they name: `slot_time`: a permutation of the time blocks in which time blocks t and t + 1 always sit in slots adjacent along tr or along tc. `diag_block`: every block is symmetric and indefinite. `precond`: every block is symmetric positive definite.
All inputs are finite; a program needn't handle non-finite values.
Results may differ from a plain program's by a relative error of at most 0.0035.
Values may be sent and summed in bfloat16 or wider, within the bound.
No kernel may reach another device: no remote copies, remote signals or barrier semaphores. Data moves between devices by JAX's collectives and lax.ppermute only.
A program may use at most 128 MiB of HBM per device.

v0:
```python
import jax
import jax.numpy as jnp
from jax import lax
from jax.sharding import PartitionSpec as P

ITERS = 3


PLACES = ((0, 1), (2, 1), (1, 0), (1, 2))


def with_halo(x, sides, width):
    for axis, dim in sides:
        count, length = (lax.axis_size(axis), x.shape[dim])
        up = [(i, (i + 1) % count) for i in range(count - 1)]
        down = [(j, i) for i, j in up]
        last = lax.slice_in_dim(x, length - width, length, axis=dim)
        first = lax.slice_in_dim(x, 0, width, axis=dim)
        before = lax.ppermute(last, axis, up)
        after = lax.ppermute(first, axis, down)
        x = jnp.concatenate([before, x, after], axis=dim)
    return x


def neighbour_pick(grid, matches):
    total = jnp.zeros_like(grid[1, 1])
    for matched, position in zip(matches, PLACES):
        total = total + jnp.where(matched, grid[position[0], position[1]], jnp.zeros_like(total))
    return total


def inner_prod(left, right):
    return jnp.sum(left * right, axis=0)


def body(diag_block, coupling, precond, rhs, slot_time):
    diag_here = diag_block[0, 0]
    coupling_here = coupling[0, 0]
    rhs_here = rhs[0, 0]
    own_time = slot_time[0, 0]
    tags = with_halo(slot_time + 1, (("tr", 0), ("tc", 1)), 1)
    before_match = [tags[p[0], p[1]] == own_time for p in PLACES]
    after_match = [tags[p[0], p[1]] == own_time + 2 for p in PLACES]
    lower = jnp.linalg.cholesky(precond[0, 0])
    lower_inv = jax.scipy.linalg.solve_triangular(
        lower, jnp.eye(lower.shape[0], dtype=jnp.float32), lower=True
    )
    inverse = jnp.dot(lower_inv.T, lower_inv, precision=lax.Precision.HIGHEST)
    contract_rows = (((0,), (0,)), ((), ()))

    def precon(resid):
        return jnp.dot(inverse, resid, precision=lax.Precision.HIGHEST)

    resid_new = rhs_here
    resid_old = jnp.zeros_like(rhs_here)
    pre_vec = precon(rhs_here)
    beta_now = jnp.sqrt(lax.psum(inner_prod(rhs_here, pre_vec), ("tr", "tc")))
    old_beta = jnp.zeros_like(beta_now)
    phi_bar = beta_now
    cosine = -jnp.ones_like(beta_now)
    sine_now = jnp.zeros_like(beta_now)
    eps_now = jnp.zeros_like(beta_now)
    d_bar = jnp.zeros_like(beta_now)
    dir_now = jnp.zeros_like(rhs_here)
    dir_old = jnp.zeros_like(rhs_here)
    solution = jnp.zeros_like(rhs_here)
    for step in range(ITERS):
        lanczos = pre_vec / beta_now
        rounded = lanczos.astype(jnp.bfloat16)
        vec_grid = with_halo(rounded[None, None], (("tr", 0), ("tc", 1)), 1)
        vec_before = neighbour_pick(vec_grid, before_match)
        own_part = jnp.dot(diag_here, rounded, preferred_element_type=jnp.float32)
        own_part = own_part + jnp.dot(coupling_here, vec_before, preferred_element_type=jnp.float32)
        back_part = lax.dot_general(
            coupling_here, rounded, contract_rows, preferred_element_type=jnp.float32
        )
        back_grid = with_halo(
            back_part[None, None].astype(jnp.bfloat16), (("tr", 0), ("tc", 1)), 1
        ).astype(jnp.float32)
        own_part = own_part + neighbour_pick(back_grid, after_match)
        image = own_part
        if step > 0:
            image = image - beta_now / old_beta * resid_old
        alpha_now = lax.psum(inner_prod(lanczos, image), ("tr", "tc"))
        resid_old = resid_new
        resid_new = image - alpha_now / beta_now * resid_new
        pre_vec = precon(resid_new)
        old_beta = beta_now
        beta_now = jnp.sqrt(lax.psum(inner_prod(resid_new, pre_vec), ("tr", "tc")))
        old_eps = eps_now
        delta_now = cosine * d_bar + sine_now * alpha_now
        g_bar = sine_now * d_bar - cosine * alpha_now
        eps_now = sine_now * beta_now
        d_bar = -cosine * beta_now
        gamma_now = jnp.sqrt(g_bar * g_bar + beta_now * beta_now)
        cosine = g_bar / gamma_now
        sine_now = beta_now / gamma_now
        phi_now = cosine * phi_bar
        phi_bar = sine_now * phi_bar
        dir_next = (lanczos - old_eps * dir_old - delta_now * dir_now) / gamma_now
        dir_old = dir_now
        dir_now = dir_next
        solution = solution + phi_now * dir_now
    return (solution[None, None], phi_bar)


def solution(mesh):
    placed = (
        P("tr", "tc", None, None),
        P("tr", "tc", None, None),
        P("tr", "tc", None, None),
        P("tr", "tc", None, None),
        P("tr", "tc"),
    )
    return jax.shard_map(
        body,
        mesh=mesh,
        in_specs=placed,
        out_specs=(P("tr", "tc", None, None), P()),
        check_vma=False,
    )
```

profile of v0, /device:TPU:1, one launch (start us, length us, event | category | flops | bytes accessed | tf_op | source)
XLA Modules:
  0.0 1107.1 jit_solution(864494820148102052)
XLA Ops:
  16.2 11.7 %cholesky.223 = f32[128,128]{1,0:T(8,128)S(1)} custom-call(f32[128,128]{1,0:T(8,128)S(1)} %cholesky.580), custom_call_target="Cholesky" | custom-call | tf_op jit(solution)/shard_map/jit(cholesky)/cholesky | solution.py:44
  28.0 9.8 custom-call.63
  44.2 11.9 %cholesky.244 = f32[128,128]{1,0:T(8,128)S(1)} custom-call(f32[128,128]{1,0:T(8,128)S(1)} %cholesky.584), custom_call_target="Cholesky" | custom-call | tf_op jit(solution)/shard_map/jit(cholesky)/cholesky | solution.py:44
  56.7 9.8 custom-call.64
  69.9 11.7 %cholesky.468 = f32[128,128]{1,0:T(8,128)S(1)} custom-call(f32[128,128]{1,0:T(8,128)S(1)} %cholesky.589), custom_call_target="Cholesky" | custom-call | tf_op jit(solution)/shard_map/jit(cholesky)/cholesky | solution.py:44
  82.9 9.8 custom-call.65
  96.2 11.9 %cholesky.487 = f32[128,128]{1,0:T(8,128)S(1)} custom-call(f32[128,128]{1,0:T(8,128)S(1)} %cholesky.594), custom_call_target="Cholesky" | custom-call | tf_op jit(solution)/shard_map/jit(cholesky)/cholesky | solution.py:44
  109.4 9.8 custom-call.66
  122.7 11.7 %cholesky.506 = f32[128,128]{1,0:T(8,128)S(1)} custom-call(f32[128,128]{1,0:T(8,128)S(1)} %cholesky.599), custom_call_target="Cholesky" | custom-call | tf_op jit(solution)/shard_map/jit(cholesky)/cholesky | solution.py:44
  135.7 10.2 custom-call.67
  149.1 11.7 %cholesky.526 = f32[128,128]{1,0:T(8,128)S(1)} custom-call(f32[128,128]{1,0:T(8,128)S(1)} %cholesky.604), custom_call_target="Cholesky" | custom-call | tf_op jit(solution)/shard_map/jit(cholesky)/cholesky | solution.py:44
  162.2 9.8 custom-call.68
  175.0 11.9 %cholesky.546 = f32[128,128]{1,0:T(8,128)S(1)} custom-call(f32[128,128]{1,0:T(8,128)S(1)} %cholesky.609), custom_call_target="Cholesky" | custom-call | tf_op jit(solution)/shard_map/jit(cholesky)/cholesky | solution.py:44
  188.1 9.8 custom-call.69
  200.5 11.7 %cholesky.564 = f32[128,128]{1,0:T(8,128)S(1)} custom-call(f32[128,128]{1,0:T(8,128)S(1)} %convolution_subtract_fusion.11), custom_call_target="Cholesky" | custom-call | tf_op jit(solution)/shard_map/jit(cholesky)/cholesky | solution.py:44
  223.8 22.6 %while.1 = (s32[]{:T(128)}, f32[1024,1024]{1,0:T(8,128)}, s32[8,2]{0,1:T(2,128)S(1)}, f32[8,128,128]{2,1,0:T(8,128)S(1)}, s32[]{:T(128)}) while((s32[]{:T(128)}, f32[1024,1024]{1,0:T(8,128)}, s32[8,2]{0,1:T(2,128)S(1)}, f32[8,128,128]{2,1,0:T(8,128)S(1)}, s32[]{:T(128)}) %tuple.84), condition=%wide.while_cond, body=%wide.while_body.sunk | while | flops 2 | bytes 131181 | solution.py:45
  246.4 78.8 %custom-call.70 = f32[8,128,128]{1,2,0:T(8,128)S(1)} custom-call(f32[8,128,128]{2,1,0:T(8,128)S(1)} %get-tuple-element.9), custom_call_target="InvertDiagBlocksLowerTriangular" | custom-call | tf_op jit(solution)/shard_map/jit(_solve_triangular)/triangular_solve | solution.py:45
  348.4 14.2 %fusion.210 = f32[1024,1024]{1,0:T(8,128)S(1)} fusion(f32[1024,1024]{1,0:T(8,128)S(1)} %convolution_dynamic-update-slice_fusion), kind=kOutput, calls=%fused_computation.331 | convolution fusion | flops 12884901888 | bytes 8388608 | tf_op jit(solution)/shard_map/dot_general | solution.py:48
  368.0 81.4 %psum.49 = f32[128]{0:T(128)S(1)} all-reduce(f32[128]{0:T(128)S(1)} %get-tuple-element.97), channel_id=1, replica_groups=mesh['tr'=16,'tc'=16] {'tr','tc'}, use_global_device_ids=true, to_apply=%region_17.18 | all-reduce | flops 128 | bytes 1024 | tf_op jit(solution)/shard_map/psum | solution.py:57
  497.8 7.1 collective-permute-done.6
  510.2 82.7 %psum.50 = f32[128]{0:T(128)S(1)} all-reduce(f32[128]{0:T(128)S(1)} %get-tuple-element.99), channel_id=1, replica_groups=mesh['tr'=16,'tc'=16] {'tr','tc'}, use_global_device_ids=true, to_apply=%region_19.20 | all-reduce | flops 128 | bytes 1024 | tf_op jit(solution)/shard_map/psum | solution.py:84
  600.1 72.7 %psum.51 = f32[128]{0:T(128)S(1)} all-reduce(f32[128]{0:T(128)S(1)} %get-tuple-element.101), channel_id=1, replica_groups=mesh['tr'=16,'tc'=16] {'tr','tc'}, use_global_device_ids=true, to_apply=%region_21.22 | all-reduce | flops 128 | bytes 1024 | tf_op jit(solution)/shard_map/psum | solution.py:89
  702.7 10.6 collective-permute-done.15
  713.3 16.8 %collective-permute-done.19 = bf16[3,1,1024,128]{3,2,1,0:T(8,128)(2,1)S(1)} collective-permute-done((bf16[3,1,1024,128]{3,2,1,0:T(8,128)(2,1)S(1)}, bf16[3,1,1024,128]{3,2,1,0:T(8,128)(2,1)S(1)}, u32[]{:S(2)}, u32[]{:S(2)}) %collective-permute-start.19) | collective-permute-done | bytes 786464 | tf_op jit(solution)/shard_map/ppermute | solution.py:20
  731.7 74.8 %psum.52 = f32[128]{0:T(128)S(1)} all-reduce(f32[128]{0:T(128)S(1)} %get-tuple-element.103), channel_id=1, replica_groups=mesh['tr'=16,'tc'=16] {'tr','tc'}, use_global_device_ids=true, to_apply=%region_23.24 | all-reduce | flops 128 | bytes 1024 | tf_op jit(solution)/shard_map/psum | solution.py:84
  808.6 6.4 multiply_reduce_fusion.1
  815.0 73.8 %psum.53 = f32[128]{0:T(128)S(1)} all-reduce(f32[128]{0:T(128)S(1)} %get-tuple-element.105), channel_id=1, replica_groups=mesh['tr'=16,'tc'=16] {'tr','tc'}, use_global_device_ids=true, to_apply=%region_25.26 | all-reduce | flops 128 | bytes 1024 | tf_op jit(solution)/shard_map/psum | solution.py:89
  920.8 10.5 collective-permute-done.23
  931.3 16.4 %collective-permute-done.27 = bf16[3,1,1024,128]{3,2,1,0:T(8,128)(2,1)S(1)} collective-permute-done((bf16[3,1,1024,128]{3,2,1,0:T(8,128)(2,1)S(1)}, bf16[3,1,1024,128]{3,2,1,0:T(8,128)(2,1)S(1)}, u32[]{:S(2)}, u32[]{:S(2)}) %collective-permute-start.27) | collective-permute-done | bytes 786464 | tf_op jit(solution)/shard_map/ppermute | solution.py:20
  949.4 75.1 %psum.54 = f32[128]{0:T(128)S(1)} all-reduce(f32[128]{0:T(128)S(1)} %get-tuple-element.107), channel_id=1, replica_groups=mesh['tr'=16,'tc'=16] {'tr','tc'}, use_global_device_ids=true, to_apply=%region_27.28 | all-reduce | flops 128 | bytes 1024 | tf_op jit(solution)/shard_map/psum | solution.py:84
  1024.5 5.9 fusion.81
  1030.4 73.6 %psum.55 = f32[128]{0:T(128)S(1)} all-reduce(f32[128]{0:T(128)S(1)} %fusion.81), channel_id=1, replica_groups=mesh['tr'=16,'tc'=16] {'tr','tc'}, use_global_device_ids=true, to_apply=%region_29.30 | all-reduce | flops 128 | bytes 1024 | tf_op jit(solution)/shard_map/psum | solution.py:89
  (202 shorter events, 231.0 us)
Async XLA Ops:
  0.6 452.8 %copy-start = (bf16[1,1,1024,1024]{3,2,1,0:T(8,128)(2,1)S(1)}, bf16[1,1,1024,1024]{3,2,1,0:T(8,128)(2,1)}, u32[]{:S(2)}) copy-start(bf16[1,1,1024,1024]{3,2,1,0:T(8,128)(2,1)} %param.6) | copy-start | bytes 6291460
  449.5 10.2 collective-permute-start.1
  452.1 8.6 collective-permute-start.3
  454.3 13.4 %collective-permute-start.8 = (bf16[1,1,1024,128]{3,2,1,0:T(8,128)(2,1)S(1)}, bf16[1,1,1024,128]{3,2,1,0:T(8,128)(2,1)S(1)}, u32[]{:S(2)}, u32[]{:S(2)}) collective-permute-start(bf16[1,1,1024,128]{3,2,1,0:T(8,128)(2,1)S(1)} %fusion.88), channel_id=1, source_target_pairs={{0,16},{16,32},{32,48},{48,64},{64,80},{80,96},{96,112},{112,128},... | collective-permute-start | bytes 786440 | tf_op jit(solution)/shard_map/ppermute | solution.py:19
  458.3 9.5 collective-permute-start.9
  461.6 45.4 %collective-permute-start.5 = (bf16[3,1,1024,128]{3,2,1,0:T(8,128)(2,1)}, bf16[3,1,1024,128]{3,2,1,0:T(8,128)(2,1)}, u32[]{:S(2)}, u32[]{:S(2)}) collective-permute-start(bf16[3,1,1024,128]{3,2,1,0:T(8,128)(2,1)} %pad_maximum_fusion), channel_id=1, source_target_pairs={{0,1},{1,2},{2,3},{3,4},{4,5},{5,6},{6,7},{7,8},{8,9},{9,10},{10,1... | collective-permute-start | bytes 2359304 | tf_op jit(solution)/shard_map/ppermute | solution.py:19
  464.9 42.2 %collective-permute-start.7 = (bf16[3,1,1024,128]{3,2,1,0:T(8,128)(2,1)}, bf16[3,1,1024,128]{3,2,1,0:T(8,128)(2,1)}, u32[]{:S(2)}, u32[]{:S(2)}) collective-permute-start(bf16[3,1,1024,128]{3,2,1,0:T(8,128)(2,1)} %pad_maximum_fusion), channel_id=1, source_target_pairs={{1,0},{2,1},{3,2},{4,3},{5,4},{6,5},{7,6},{8,7},{9,8},{10,9},{11,1... | collective-permute-start | bytes 2359304 | tf_op jit(solution)/shard_map/ppermute | solution.py:20
  468.9 38.1 %collective-permute-start.10 = (bf16[3,1,1024,128]{3,2,1,0:T(8,128)(2,1)}, bf16[3,1,1024,128]{3,2,1,0:T(8,128)(2,1)}, u32[]{:S(2)}, u32[]{:S(2)}) collective-permute-start(bf16[3,1,1024,128]{3,2,1,0:T(8,128)(2,1)} %pad_maximum_fusion.1), channel_id=1, source_target_pairs={{0,1},{1,2},{2,3},{3,4},{4,5},{5,6},{6,7},{7,8},{8,9},{9,10},{10,1... | collective-permute-start | bytes 2359304 | tf_op jit(solution)/shard_map/ppermute | solution.py:19
  471.6 35.5 %collective-permute-start.11 = (bf16[3,1,1024,128]{3,2,1,0:T(8,128)(2,1)}, bf16[3,1,1024,128]{3,2,1,0:T(8,128)(2,1)}, u32[]{:S(2)}, u32[]{:S(2)}) collective-permute-start(bf16[3,1,1024,128]{3,2,1,0:T(8,128)(2,1)} %pad_maximum_fusion.1), channel_id=1, source_target_pairs={{1,0},{2,1},{3,2},{4,3},{5,4},{6,5},{7,6},{8,7},{9,8},{10,9},{11,1... | collective-permute-start | bytes 2359304 | tf_op jit(solution)/shard_map/ppermute | solution.py:20
  474.8 6.7 collective-permute-start
  481.5 4.2 collective-permute-start.2
  487.1 7.5 collective-permute-start.4
  494.7 10.2 collective-permute-start.6
  672.8 11.5 %collective-permute-start.12 = (bf16[1,1,1024,128]{3,2,1,0:T(8,128)(2,1)S(1)}, bf16[1,1,1024,128]{3,2,1,0:T(8,128)(2,1)S(1)}, u32[]{:S(2)}, u32[]{:S(2)}) collective-permute-start(bf16[1,1,1024,128]{3,2,1,0:T(8,128)(2,1)S(1)} %convert_bitcast_fusion.1), channel_id=1, source_target_pairs={{0,16},{16,32},{32,48},{48,64},{64,80},{80,96},{96,112},{112,128},... | collective-permute-start | bytes 786440 | tf_op jit(solution)/shard_map/ppermute | solution.py:19
  676.7 8.8 collective-permute-start.13
  678.9 51.1 %copy-start.9 = (f32[1,1,1024,128]{3,2,1,0:T(8,128)S(1)}, f32[1,1,1024,128]{3,2,1,0:T(8,128)}, u32[]{:S(2)}) copy-start(f32[1,1,1024,128]{3,2,1,0:T(8,128)} %param.8) | copy-start | bytes 1572868
  678.9 13.2 %collective-permute-start.16 = (bf16[1,1,1024,128]{3,2,1,0:T(8,128)(2,1)S(1)}, bf16[1,1,1024,128]{3,2,1,0:T(8,128)(2,1)S(1)}, u32[]{:S(2)}, u32[]{:S(2)}) collective-permute-start(bf16[1,1,1024,128]{3,2,1,0:T(8,128)(2,1)S(1)} %fusion.85), channel_id=1, source_target_pairs={{0,16},{16,32},{32,48},{48,64},{64,80},{80,96},{96,112},{112,128},... | collective-permute-start | bytes 786440 | tf_op jit(solution)/shard_map/ppermute | solution.py:19
  683.1 9.1 collective-permute-start.17
  685.5 17.2 %collective-permute-start.14 = (bf16[3,1,1024,128]{3,2,1,0:T(8,128)(2,1)S(1)}, bf16[3,1,1024,128]{3,2,1,0:T(8,128)(2,1)S(1)}, u32[]{:S(2)}, u32[]{:S(2)}) collective-permute-start(bf16[3,1,1024,128]{3,2,1,0:T(8,128)(2,1)S(1)} %pad_maximum_fusion.2), channel_id=1, source_target_pairs={{0,1},{1,2},{2,3},{3,4},{4,5},{5,6},{6,7},{7,8},{8,9},{9,10},{10,1... | collective-permute-start | bytes 2359304 | tf_op jit(solution)/shard_map/ppermute | solution.py:19
  690.2 23.1 %collective-permute-start.15 = (bf16[3,1,1024,128]{3,2,1,0:T(8,128)(2,1)S(1)}, bf16[3,1,1024,128]{3,2,1,0:T(8,128)(2,1)S(1)}, u32[]{:S(2)}, u32[]{:S(2)}) collective-permute-start(bf16[3,1,1024,128]{3,2,1,0:T(8,128)(2,1)S(1)} %pad_maximum_fusion.2), channel_id=1, source_target_pairs={{1,0},{2,1},{3,2},{4,3},{5,4},{6,5},{7,6},{8,7},{9,8},{10,9},{11,1... | collective-permute-start | bytes 2359304 | tf_op jit(solution)/shard_map/ppermute | solution.py:20
  692.2 21.0 %collective-permute-start.18 = (bf16[3,1,1024,128]{3,2,1,0:T(8,128)(2,1)S(1)}, bf16[3,1,1024,128]{3,2,1,0:T(8,128)(2,1)S(1)}, u32[]{:S(2)}, u32[]{:S(2)}) collective-permute-start(bf16[3,1,1024,128]{3,2,1,0:T(8,128)(2,1)S(1)} %pad_maximum_fusion.3), channel_id=1, source_target_pairs={{0,1},{1,2},{2,3},{3,4},{4,5},{5,6},{6,7},{7,8},{8,9},{9,10},{10,1... | collective-permute-start | bytes 2359304 | tf_op jit(solution)/shard_map/ppermute | solution.py:19
  696.6 33.5 %collective-permute-start.19 = (bf16[3,1,1024,128]{3,2,1,0:T(8,128)(2,1)S(1)}, bf16[3,1,1024,128]{3,2,1,0:T(8,128)(2,1)S(1)}, u32[]{:S(2)}, u32[]{:S(2)}) collective-permute-start(bf16[3,1,1024,128]{3,2,1,0:T(8,128)(2,1)S(1)} %pad_maximum_fusion.3), channel_id=1, source_target_pairs={{1,0},{2,1},{3,2},{4,3},{5,4},{6,5},{7,6},{8,7},{9,8},{10,9},{11,1... | collective-permute-start | bytes 2359304 | tf_op jit(solution)/shard_map/ppermute | solution.py:20
  888.8 26.9 %copy-start.15 = (bf16[1,1,1024,1024]{3,2,1,0:T(8,128)(2,1)S(1)}, bf16[1,1,1024,1024]{3,2,1,0:T(8,128)(2,1)}, u32[]{:S(2)}) copy-start(bf16[1,1,1024,1024]{3,2,1,0:T(8,128)(2,1)} %param.5) | copy-start | bytes 6291460
  890.0 11.6 %collective-permute-start.20 = (bf16[1,1,1024,128]{3,2,1,0:T(8,128)(2,1)S(1)}, bf16[1,1,1024,128]{3,2,1,0:T(8,128)(2,1)S(1)}, u32[]{:S(2)}, u32[]{:S(2)}) collective-permute-start(bf16[1,1,1024,128]{3,2,1,0:T(8,128)(2,1)S(1)} %convert_bitcast_fusion), channel_id=1, source_target_pairs={{0,16},{16,32},{32,48},{48,64},{64,80},{80,96},{96,112},{112,128},... | collective-permute-start | bytes 786440 | tf_op jit(solution)/shard_map/ppermute | solution.py:19
  892.9 8.8 collective-permute-start.21
  896.2 51.5 %copy-start.6 = (f32[1024,128]{1,0:T(8,128)S(1)}, f32[1024,128]{1,0:T(8,128)}, u32[]{:S(2)}) copy-start(f32[1024,128]{1,0:T(8,128)} %copy-done.5) | copy-start | bytes 1572868
  896.2 12.0 %collective-permute-start.24 = (bf16[1,1,1024,128]{3,2,1,0:T(8,128)(2,1)S(1)}, bf16[1,1,1024,128]{3,2,1,0:T(8,128)(2,1)S(1)}, u32[]{:S(2)}, u32[]{:S(2)}) collective-permute-start(bf16[1,1,1024,128]{3,2,1,0:T(8,128)(2,1)S(1)} %fusion.82), channel_id=1, source_target_pairs={{0,16},{16,32},{32,48},{48,64},{64,80},{80,96},{96,112},{112,128},... | collective-permute-start | bytes 786440 | tf_op jit(solution)/shard_map/ppermute | solution.py:19
  900.3 8.2 collective-permute-start.25
  901.7 19.0 %collective-permute-start.22 = (bf16[3,1,1024,128]{3,2,1,0:T(8,128)(2,1)S(1)}, bf16[3,1,1024,128]{3,2,1,0:T(8,128)(2,1)S(1)}, u32[]{:S(2)}, u32[]{:S(2)}) collective-permute-start(bf16[3,1,1024,128]{3,2,1,0:T(8,128)(2,1)S(1)} %pad_maximum_fusion.4), channel_id=1, source_target_pairs={{0,1},{1,2},{2,3},{3,4},{4,5},{5,6},{6,7},{7,8},{8,9},{9,10},{10,1... | collective-permute-start | bytes 2359304 | tf_op jit(solution)/shard_map/ppermute | solution.py:19
  906.2 25.0 %collective-permute-start.23 = (bf16[3,1,1024,128]{3,2,1,0:T(8,128)(2,1)S(1)}, bf16[3,1,1024,128]{3,2,1,0:T(8,128)(2,1)S(1)}, u32[]{:S(2)}, u32[]{:S(2)}) collective-permute-start(bf16[3,1,1024,128]{3,2,1,0:T(8,128)(2,1)S(1)} %pad_maximum_fusion.4), channel_id=1, source_target_pairs={{1,0},{2,1},{3,2},{4,3},{5,4},{6,5},{7,6},{8,7},{9,8},{10,9},{11,1... | collective-permute-start | bytes 2359304 | tf_op jit(solution)/shard_map/ppermute | solution.py:20
  908.6 22.7 %collective-permute-start.26 = (bf16[3,1,1024,128]{3,2,1,0:T(8,128)(2,1)S(1)}, bf16[3,1,1024,128]{3,2,1,0:T(8,128)(2,1)S(1)}, u32[]{:S(2)}, u32[]{:S(2)}) collective-permute-start(bf16[3,1,1024,128]{3,2,1,0:T(8,128)(2,1)S(1)} %pad_maximum_fusion.5), channel_id=1, source_target_pairs={{0,1},{1,2},{2,3},{3,4},{4,5},{5,6},{6,7},{7,8},{8,9},{9,10},{10,1... | collective-permute-start | bytes 2359304 | tf_op jit(solution)/shard_map/ppermute | solution.py:19
  913.7 34.0 %collective-permute-start.27 = (bf16[3,1,1024,128]{3,2,1,0:T(8,128)(2,1)S(1)}, bf16[3,1,1024,128]{3,2,1,0:T(8,128)(2,1)S(1)}, u32[]{:S(2)}, u32[]{:S(2)}) collective-permute-start(bf16[3,1,1024,128]{3,2,1,0:T(8,128)(2,1)S(1)} %pad_maximum_fusion.5), channel_id=1, source_target_pairs={{1,0},{2,1},{3,2},{4,3},{5,4},{6,5},{7,6},{8,7},{9,8},{10,9},{11,1... | collective-permute-start | bytes 2359304 | tf_op jit(solution)/shard_map/ppermute | solution.py:20
  (12 other events, 97.6 us)
where the time goes:
time: 1120 us; the launch traced here: 1110 us
  blocking collectives  534 us (48%)
  other arithmetic  274 us (24%)
  matrix products  96.2 us (9%)
  starting transfers between devices  78.8 us (7%)
  waiting for transfers between devices  74.5 us (7%)
  local copies, waits for them, and re-layouts  37 us (3%)
  between operations  12.2 us (1%)
    psum x3, blocking collectives, body(): alpha_now = lax.psum(inner_prod(lanczos, image), ('tr', 'tc'))  233 us
    psum x3, blocking collectives, body(): beta_now = jnp.sqrt(lax.psum(inner_prod(resid_new, pre_vec), ('tr', 'tc')))  220 us
    another operation x30, other arithmetic, body(): lower = jnp.linalg.cholesky(precond[0, 0])  172 us
    another operation x3, other arithmetic, body(): jax.scipy.linalg.solve_triangular(lower, jnp.eye(lower.shape[0], dtype=jn...  83.6 us
    psum x1, blocking collectives, body(): beta_now = jnp.sqrt(lax.psum(inner_prod(rhs_here, pre_vec), ('tr', 'tc')))  81.4 us
    ppermute x14, waiting for transfers between devices, with_halo(): after = lax.ppermute(first, axis, down)  66.6 us
    ppermute x14, starting transfers between devices, with_halo(): before = lax.ppermute(last, axis, up)  54.6 us
    ppermute x14, starting transfers between devices, with_halo(): after = lax.ppermute(first, axis, down)  24.1 us
  transfers between devices with their start and end apart: 28, of which 11 were waited for; matrix products, arithmetic and copies ran while one was open for 1% of the time, Pallas kernels for 0%

commit v1 on v0

v1 whole, which is shorter than its diff:
```python
import functools

import jax
import jax.numpy as jnp
from jax import lax
from jax.experimental import pallas as pl
from jax.experimental.pallas import tpu as pltpu
from jax.sharding import PartitionSpec as P

ITERS = 3
BASIS = ITERS + 1
PAIRS = tuple((i, j) for i in range(BASIS) for j in range(i, BASIS))
LEAF = 256
F32 = jnp.float32
BF16 = jnp.bfloat16
MIB = 2**20


def vmem():
    return pl.BlockSpec(memory_space=pltpu.VMEM)


def smem():
    return pl.BlockSpec(memory_space=pltpu.SMEM)


def pinned(x):
    return pltpu.with_memory_space_constraint(x, pltpu.VMEM)


def params(mib):
    return pltpu.CompilerParams(vmem_limit_bytes=mib * MIB)


def mm(a, b):
    return lax.dot_general(a, b, (((1,), (0,)), ((), ())), preferred_element_type=F32)


def tn(a, b):
    return lax.dot_general(a, b, (((0,), (0,)), ((), ())), preferred_element_type=F32)


def split(x):
    high = x.astype(BF16)
    return high, (x - high.astype(F32)).astype(BF16)


def mm3(a, b):
    return mm(a[0], b[0]) + (mm(a[0], b[1]) + mm(a[1], b[0]))


def tn3(a, b):
    return tn(a[0], b[0]) + (tn(a[0], b[1]) + tn(a[1], b[0]))


def column_norm(x):
    return jnp.max(jnp.sum(jnp.abs(x), axis=0, keepdims=True), axis=1, keepdims=True)


def pivot_inverse(block):
    n = block.shape[0]
    rows = lax.broadcasted_iota(jnp.int32, (n, n), 0)
    cols = lax.broadcasted_iota(jnp.int32, (n, n), 1)
    eye = jnp.where(rows == cols, 1.0, 0.0).astype(F32)
    alpha = 1.8 / column_norm(block)
    parts = split(block)
    power = eye - alpha * block
    inv = alpha * (eye + power)
    power = power.astype(BF16)
    for _ in range(4):
        power = mm(power, power).astype(BF16)
        inv = inv + mm(inv.astype(BF16), power)
    high = inv.astype(BF16)
    resid = eye - (mm(parts[0], high) + mm(parts[1], high))
    inv = high.astype(F32) + mm(high, resid.astype(BF16))
    inv_parts = split(inv)
    resid = eye - mm3(parts, inv_parts)
    inv = inv + mm(inv_parts[0], resid.astype(BF16))

    def unfinished(carry):
        return jnp.logical_and(carry[2] > 5e-3, carry[0] < 80)

    def refine(carry):
        count, x, _ = carry
        error = eye - jnp.dot(block, x, precision=lax.Precision.HIGHEST)
        x = x + jnp.dot(x, error, precision=lax.Precision.HIGHEST)
        return count + 1, x, jnp.max(column_norm(error))

    return lax.while_loop(
        unfinished, refine, (jnp.int32(0), inv, jnp.max(column_norm(resid)))
    )[1]


def store_applied(out_ref, high_ref, low_ref, vec_ref):
    high, low = split(vec_ref[...])
    both = jnp.concatenate([high, low], axis=1)
    width = high.shape[1]
    for k in range(0, out_ref.shape[0], LEAF):
        rows = pl.ds(k, LEAF)
        part = mm(high_ref[rows, :], both)
        out_ref[rows, :] = part[:, :width] + (part[:, width:] + mm(low_ref[rows, :], high))


def inverse_kernel(p_ref, rhs_ref, c_ref, high_ref, low_ref, ct_ref, vec_ref, size_ref, work, scale):
    n = p_ref.shape[0]
    rows = lax.broadcasted_iota(jnp.int32, (128, 128), 0)
    cols = lax.broadcasted_iota(jnp.int32, (128, 128), 1)
    lanes = []
    for k in range(0, n, 128):
        at = pl.ds(k, 128)
        diag = jnp.where(rows == cols, p_ref[at, at], 0.0)
        scale[at, :] = jnp.broadcast_to(lax.rsqrt(jnp.sum(diag, axis=1, keepdims=True)), (128, 128))
        lanes.append(lax.rsqrt(jnp.sum(diag, axis=0, keepdims=True)))
    lanes = jnp.concatenate(lanes, axis=1)
    starts = range(0, n, LEAF)
    for k in starts:
        at = pl.ds(k, LEAF)
        work[at, :] = p_ref[at, :] * scale[at, :][:, :1] * lanes
    for k in starts:
        at = pl.ds(k, LEAF)
        pivot = pivot_inverse(work[at, at])
        pivot_parts = split(pivot)
        old, new = {}, {}
        for j in starts:
            if j != k:
                old[j] = split(work[at, pl.ds(j, LEAF)])
                row = mm3(pivot_parts, old[j])
                new[j] = split(row)
                work[at, pl.ds(j, LEAF)] = row
        for i in old:
            for j in old:
                spot = (pl.ds(i, LEAF), pl.ds(j, LEAF))
                work[spot] = work[spot] - tn3(old[i], new[j])
            work[pl.ds(i, LEAF), at] = work[at, pl.ds(i, LEAF)].T
        work[at, at] = -pivot
    largest = jnp.zeros((1, 1), F32)
    for k in starts:
        at = pl.ds(k, LEAF)
        inv = -(work[at, :] * scale[at, :][:, :1] * lanes)
        high_ref[at, :], low_ref[at, :] = split(inv)
        largest = jnp.maximum(largest, jnp.max(jnp.max(jnp.abs(inv), axis=0, keepdims=True), axis=1, keepdims=True))
        ct_ref[:, at] = c_ref[at, :].T
    size_ref[...] = jnp.broadcast_to(largest, size_ref.shape)
    store_applied(vec_ref, high_ref, low_ref, rhs_ref)


def invert(precond, rhs, coupling):
    n, width = rhs.shape
    return pl.pallas_call(
        inverse_kernel,
        out_shape=[
            pltpu.VMEM((n, n), BF16),
            pltpu.VMEM((n, n), BF16),
            pltpu.VMEM((n, n), BF16),
            pltpu.VMEM((n, width), F32),
            pltpu.VMEM((8, width), F32),
        ],
        in_specs=[vmem()] * 3,
        out_specs=[vmem()] * 5,
        scratch_shapes=[pltpu.VMEM((n, n), F32), pltpu.VMEM((n, 128), F32)],
        compiler_params=params(32),
    )(pinned(precond), pinned(rhs), pinned(coupling))


def write_messages(flags, ct_ref, vec_ref, out_refs):
    high = vec_ref[...].astype(BF16)
    for k in range(0, vec_ref.shape[0], LEAF):
        rows = pl.ds(k, LEAF)
        back = mm(ct_ref[rows, :], high).astype(BF16)
        ahead = high[k:k + LEAF, :]
        for d, out in enumerate(out_refs):
            out[rows, :] = jnp.where(flags[d] == 1, ahead, jnp.where(flags[4 + d] == 1, back, jnp.zeros_like(back)))


def message_kernel(flags, ct_ref, vec_ref, *out_refs):
    write_messages(flags, ct_ref, vec_ref, out_refs)


def own_kernel(diag_ref, vec_ref, out_ref):
    both = jnp.concatenate(split(vec_ref[...]), axis=1)
    width = vec_ref.shape[1]
    for k in range(0, out_ref.shape[0], LEAF):
        rows = pl.ds(k, LEAF)
        part = mm(diag_ref[rows, :], both)
        out_ref[rows, :] = part[:, :width] + part[:, width:]


def residual_rows(flags, own_ref, c_ref, got, out_ref):
    zero = jnp.zeros(got[0].shape, BF16)
    before = zero
    for d, ref in enumerate(got):
        before = jnp.where(flags[4 + d] == 1, ref[...], before)
    for k in range(0, out_ref.shape[0], LEAF):
        rows = pl.ds(k, LEAF)
        after = zero[:LEAF]
        for d, ref in enumerate(got):
            after = jnp.where(flags[d] == 1, ref[rows, :], after)
        out_ref[rows, :] = own_ref[rows, :] + mm(c_ref[rows, :], before) + after.astype(F32)


def step_kernel(flags, own_ref, c_ref, ct_ref, high_ref, low_ref, g0, g1, g2, g3, res_ref, vec_ref, *out_refs):
    residual_rows(flags, own_ref, c_ref, (g0, g1, g2, g3), res_ref)
    store_applied(vec_ref, high_ref, low_ref, res_ref)
    write_messages(flags, ct_ref, vec_ref, out_refs)


def last_kernel(flags, own_ref, c_ref, high_ref, low_ref, size_ref, r0, p0, r1, p1, r2, p2, g0, g1, g2, g3, out_ref, r3, p3):
    residual_rows(flags, own_ref, c_ref, (g0, g1, g2, g3), r3)
    store_applied(p3, high_ref, low_ref, r3)
    res = (r0, r1, r2, r3)
    vec = (p0, p1, p2, p3)
    unit = size_ref[0:1, :]
    sizes = [jnp.maximum(jnp.max(jnp.abs(r[...]), axis=0, keepdims=True), 1e-30) for r in res]
    rows = [jnp.zeros_like(unit)] * len(PAIRS)
    for k in range(0, r3.shape[0], LEAF):
        at = pl.ds(k, LEAF)
        left = [res[i][at, :] / sizes[i] for i in range(BASIS)]
        right = [vec[i][at, :] / (sizes[i] * unit) for i in range(BASIS)]
        for m, (i, j) in enumerate(PAIRS):
            rows[m] = rows[m] + jnp.sum(left[i] * right[j], axis=0, keepdims=True)
    rows = rows + sizes + [unit]
    rows = rows + [jnp.zeros_like(unit)] * (16 - len(rows))
    packed = jnp.concatenate(rows, axis=0)
    for d in range(out_ref.shape[0]):
        out_ref[d] = packed


def merge(got):
    count = len(PAIRS)
    sizes = [jnp.max(got[:, count + i, :], axis=0, keepdims=True) for i in range(BASIS)]
    unit = jnp.max(got[:, count + BASIS, :], axis=0, keepdims=True)
    share = [got[:, count + i, :] / sizes[i] for i in range(BASIS)]
    unit_share = got[:, count + BASIS, :] / unit
    rows = []
    for m, (i, j) in enumerate(PAIRS):
        rows.append(jnp.sum(got[:, m, :] * (share[i] * share[j] * unit_share), axis=0, keepdims=True))
    return rows, sizes, unit


def merge_kernel(in_ref, out_ref):
    rows, sizes, unit = merge(in_ref[...])
    rows = rows + sizes + [unit]
    rows = rows + [jnp.zeros_like(unit)] * (16 - len(rows))
    packed = jnp.concatenate(rows, axis=0)
    for d in range(out_ref.shape[0]):
        out_ref[d] = packed


def recurrence(rows, sizes, unit):
    gram = {}
    for m, (i, j) in enumerate(PAIRS):
        gram[i, j] = gram[j, i] = rows[m]
    lead = sizes[1] / sizes[0]
    grow = [sizes[j + 1] / sizes[j] / lead for j in range(ITERS)]
    zero = jnp.zeros_like(unit)

    def dot(a, b):
        return sum(a[i] * b[j] * gram[i, j] for i in a for j in b)

    def axpy(a, x, y):
        out = {i: a * v for i, v in x.items()}
        for i, v in y.items():
            out[i] = out[i] + v if i in out else v
        return out

    resid_new = {0: jnp.ones_like(unit)}
    resid_old = {}
    beta_now = jnp.sqrt(dot(resid_new, resid_new))
    old_beta = zero
    phi_bar = beta_now
    cosine = -jnp.ones_like(unit)
    sine_now = eps_now = d_bar = zero
    dir_now, dir_old, total = {}, {}, {}
    for step in range(ITERS):
        lanczos = {i: v / beta_now for i, v in resid_new.items()}
        image = {i + 1: v * grow[i] for i, v in lanczos.items()}
        if step > 0:
            image = axpy(-beta_now / old_beta, resid_old, image)
        alpha_now = dot(lanczos, image)
        resid_old = resid_new
        resid_new = axpy(-alpha_now / beta_now, resid_new, image)
        old_beta = beta_now
        beta_now = jnp.sqrt(dot(resid_new, resid_new))
        old_eps = eps_now
        delta_now = cosine * d_bar + sine_now * alpha_now
        g_bar = sine_now * d_bar - cosine * alpha_now
        eps_now = sine_now * beta_now
        d_bar = -cosine * beta_now
        gamma_now = jnp.sqrt(g_bar * g_bar + beta_now * beta_now)
        cosine = g_bar / gamma_now
        sine_now = beta_now / gamma_now
        phi_now = cosine * phi_bar
        phi_bar = sine_now * phi_bar
        dir_next = axpy(-old_eps, dir_old, axpy(-delta_now, dir_now, lanczos))
        dir_next = {i: v / gamma_now for i, v in dir_next.items()}
        dir_old, dir_now = dir_now, dir_next
        total = axpy(phi_now, dir_now, total)
    coefs = [total[i] * (sizes[0] / sizes[i]) / lead for i in range(ITERS)]
    return coefs, phi_bar * sizes[0] * jnp.sqrt(unit)


def finish_kernel(in_ref, p0, p1, p2, out_ref, norm_ref):
    coefs, norm = recurrence(*merge(in_ref[...]))
    norm_ref[...] = norm
    for k in range(0, out_ref.shape[0], LEAF):
        at = pl.ds(k, LEAF)
        out_ref[at, :] = coefs[0] * p0[at, :] + coefs[1] * p1[at, :] + coefs[2] * p2[at, :]


def neighbour_perms(count):
    even = [(i, i ^ 1) for i in range(count)]
    odd = [(i, i + 1) for i in range(1, count - 1, 2)]
    return even, odd + [(j, i) for i, j in odd]


def exchange(values):
    even_r, odd_r = neighbour_perms(lax.axis_size("tr"))
    even_c, odd_c = neighbour_perms(lax.axis_size("tc"))
    return [
        lax.ppermute(values[0], "tr", odd_r),
        lax.ppermute(values[1], "tc", odd_c),
        lax.ppermute(values[2], "tr", even_r),
        lax.ppermute(values[3], "tc", even_c),
    ]


def body(diag_block, coupling, precond, rhs, slot_time):
    diag_here = diag_block[0, 0]
    coupling_here = coupling[0, 0]
    rhs_here = rhs[0, 0]
    n, width = rhs_here.shape
    tags = exchange([slot_time + 1] * 4)
    own_time = slot_time[0, 0]
    tags = jnp.concatenate([t.reshape(1) for t in tags])
    flags = jnp.concatenate([tags == own_time + 2, tags == own_time]).astype(jnp.int32)
    whole = jax.ShapeDtypeStruct((n, width), F32)
    sent = [jax.ShapeDtypeStruct((n, width), BF16)] * 4

    high, low, flipped, vec, size = invert(precond[0, 0], rhs_here, coupling_here)
    messages = pl.pallas_call(
        message_kernel,
        out_shape=sent,
        in_specs=[smem(), vmem(), vmem()],
        out_specs=[vmem()] * 4,
        compiler_params=params(8),
    )(flags, pinned(flipped), pinned(vec))
    basis = [rhs_here, vec]
    for step in range(ITERS):
        got = exchange(messages)
        own = pl.pallas_call(
            own_kernel,
            out_shape=pltpu.VMEM((n, width), F32),
            in_specs=[vmem()] * 2,
            out_specs=vmem(),
            compiler_params=params(8),
        )(pinned(diag_here), pinned(vec))
        if step < ITERS - 1:
            out = pl.pallas_call(
                step_kernel,
                out_shape=[pltpu.VMEM((n, width), F32)] * 2 + sent,
                in_specs=[smem()] + [vmem()] * 9,
                out_specs=[vmem()] * 6,
                compiler_params=params(12),
            )(flags, pinned(own), pinned(coupling_here), pinned(flipped), pinned(high), pinned(low), *got)
            vec = out[1]
            basis += [out[0], vec]
            messages = out[2:]
    count = lax.axis_size("tc")
    part = pl.pallas_call(
        last_kernel,
        out_shape=jax.ShapeDtypeStruct((count, 16, width), F32),
        in_specs=[smem()] + [vmem()] * 15,
        out_specs=vmem(),
        scratch_shapes=[pltpu.VMEM((n, width), F32)] * 2,
        compiler_params=params(12),
    )(flags, pinned(own), pinned(coupling_here), pinned(high), pinned(low), pinned(size), *[pinned(b) for b in basis], *got)
    part = lax.all_to_all(part, "tc", 0, 0, tiled=True)
    part = pl.pallas_call(
        merge_kernel,
        out_shape=jax.ShapeDtypeStruct((lax.axis_size("tr"), 16, width), F32),
        in_specs=[vmem()],
        out_specs=vmem(),
    )(part)
    part = lax.all_to_all(part, "tr", 0, 0, tiled=True)
    solution, norm = pl.pallas_call(
        finish_kernel,
        out_shape=[whole, jax.ShapeDtypeStruct((1, width), F32)],
        in_specs=[vmem()] * 4,
        out_specs=[vmem()] * 2,
        compiler_params=params(8),
    )(part, pinned(basis[1]), pinned(basis[3]), pinned(basis[5]))
    return (solution[None, None], norm[0])


def solution(mesh):
    placed = (
        P("tr", "tc", None, None),
        P("tr", "tc", None, None),
        P("tr", "tc", None, None),
        P("tr", "tc", None, None),
        P("tr", "tc"),
    )
    return jax.shard_map(
        body,
        mesh=mesh,
        in_specs=placed,
        out_specs=(P("tr", "tc", None, None), P()),
        check_vma=False,
    )
```

time: 1120 us -> 128 us (0.11); the launches traced: 1110 us -> 127 us
  blocking collectives: 534 us -> 36.5 us
  other arithmetic: 274 us -> 2.92 us
  matrix products: 96.2 us -> 0 us
  waiting for transfers between devices: 74.5 us -> 9.07 us
  starting transfers between devices: 78.8 us -> 40.8 us
  local copies, waits for them, and re-layouts: 37 us -> 4.83 us
  Pallas kernels: 0 us -> 31.2 us
    psum x7 -> x0, blocking collectives: 534 us -> none  [the longest x3 233 us: body(): alpha_now = lax.psum(inner_prod(lanczos, image), ('tr', 'tc'))]
    another operation x33 -> x0, other arithmetic: 256 us -> none  [the longest x30 172 us: body(): lower = jnp.linalg.cholesky(precond[0, 0])]
    ppermute x28 -> x16, waiting for transfers between devices: 74.5 us -> 9.07 us  [the longest x4 8.97 us: exchange(): lax.ppermute(values[2], 'tr', even_r)]
    dot_general x14 -> x0, matrix products: 50.1 us -> none  [the longest x4 21 us: precon(): return jnp.dot(inverse, resid, precision=lax.Precision.HIGHEST)]
    another operation x29 -> x0, matrix products: 46.1 us -> none  [the longest x14 23.1 us: body(): lower = jnp.linalg.cholesky(precond[0, 0])]
    ppermute x28 -> x16, starting transfers between devices: 78.8 us -> 40.8 us  [the longest x4 19 us: exchange(): lax.ppermute(values[2], 'tr', even_r)]
    all_to_all x0 -> x2, blocking collectives: none -> 36.5 us  [the longest x1 19.2 us: body(): part = lax.all_to_all(part, 'tr', 0, 0, tiled=True)]
    pallas_call x0 -> x10, Pallas kernels: none -> 31.2 us  [the longest x1 16 us: invert(): pl.pallas_call(inverse_kernel, out_shape=[pltpu.VMEM((n, n), BF16), pltpu...]
  transfers between devices with their start and end apart: 28 -> 16, of which waited for: 11 -> 4; matrix products, arithmetic and copies ran while one was open for 1% -> 0% of each run, Pallas kernels for 0% -> 14%
where the time goes in v1:
time: 128 us; the launch traced here: 127 us
  starting transfers between devices  40.8 us (32%)
  blocking collectives  36.5 us (29%)
  Pallas kernels  31.2 us (24%)
  waiting for transfers between devices  9.07 us (7%)
  local copies, waits for them, and re-layouts  4.83 us (4%)
  other arithmetic  2.92 us (2%)
  between operations  1.48 us (1%)
    all_to_all x1, blocking collectives, body(): part = lax.all_to_all(part, 'tr', 0, 0, tiled=True)  19.2 us
    ppermute x4, starting transfers between devices, exchange(): lax.ppermute(values[2], 'tr', even_r)  19 us
    all_to_all x1, blocking collectives, body(): part = lax.all_to_all(part, 'tc', 0, 0, tiled=True)  17.3 us
    pallas_call x1, Pallas kernels, invert(): pl.pallas_call(inverse_kernel, out_shape=[pltpu.VMEM((n, n), BF16), pltpu...  16 us
    ppermute x4, starting transfers between devices, exchange(): lax.ppermute(values[1], 'tc', odd_c)  14.4 us
    ppermute x4, waiting for transfers between devices, exchange(): lax.ppermute(values[2], 'tr', even_r)  8.97 us
    pallas_call x2, Pallas kernels, body(): pl.pallas_call(step_kernel, out_shape=[pltpu.VMEM((n, width), F32)] * 2 +...  6.11 us
    unnamed x8, local copies, waits for them, and re-layouts  4.83 us
  transfers between devices with their start and end apart: 16, of which 4 were waited for; matrix products, arithmetic and copies ran while one was open for 0% of the time, Pallas kernels for 14%

profile of v1, /device:TPU:1, one launch (start us, length us, event | category | flops | bytes accessed | tf_op | source)
XLA Modules:
  0.0 126.8 jit_solution(10529739238886695380)
XLA Ops:
  1.3 4.1 %collective-permute-start.3 = (s32[1,1]{1,0:T(1,128)}, s32[1,1]{1,0:T(1,128)}, u32[]{:S(2)}, u32[]{:S(2)}) collective-permute-start(s32[1,1]{1,0:T(1,128)} %add.6), channel_id=1, source_target_pairs={{0,1},{1,0},{2,3},{3,2},{4,5},{5,4},{6,7},{7,6},{8,9},{9,8},{10,11... | collective-permute-start | bytes 20 | tf_op jit(solution)/shard_map/ppermute | solution.py:323
  5.4 0.7 collective-permute-start.2
  6.2 4.5 %collective-permute-start.1 = (s32[1,1]{1,0:T(1,128)}, s32[1,1]{1,0:T(1,128)}, u32[]{:S(2)}, u32[]{:S(2)}) collective-permute-start(s32[1,1]{1,0:T(1,128)} %add.6), channel_id=1, source_target_pairs={{1,2},{3,4},{5,6},{7,8},{9,10},{11,12},{13,14},{2,1},{4,3},{6,5},{... | collective-permute-start | bytes 20 | tf_op jit(solution)/shard_map/ppermute | solution.py:321
  10.6 1.2 collective-permute-start
  11.9 1.6 %copy-done = bf16[1,1,1024,1024]{3,2,1,0:T(8,128)(2,1)S(1)} copy-done((bf16[1,1,1024,1024]{3,2,1,0:T(8,128)(2,1)S(1)}, bf16[1,1,1024,1024]{3,2,1,0:T(8,128)(2,1)}, u32[]{:S(2)}) %copy-start) | copy-done | bytes 2097176
  13.4 2.2 %copy-done.2 = f32[1,1,1024,1024]{3,2,1,0:T(8,128)S(1)} copy-done((f32[1,1,1024,1024]{3,2,1,0:T(8,128)S(1)}, f32[1,1,1024,1024]{3,2,1,0:T(8,128)}, u32[]{:S(2)}) %copy-start.2) | copy-done | bytes 4194328
  15.6 1.0 copy-done.3
  16.7 16.0 %shard_map.68 = (bf16[1024,1024]{1,0:T(8,128)(2,1)S(1)}, bf16[1024,1024]{1,0:T(8,128)(2,1)S(1)}, bf16[1024,1024]{1,0:T(8,128)(2,1)S(1)}, f32[1024,128]{1,0:T(8,128)S(1)}, f32[8,128]{1,0:T(8,128)S(1)}) custom-call(f32[1024,1024]{1,0:T(8,128)S(1)} %bitcast.20, f32[1024,128]{1,0:T(8,128)S(1)} %bitcast.21, bf16[1024,1024]{1,0:T(8,128)(2,1)S(1)} %bitcast.13), custom_call_target="tpu_custom_call" | custom-call | tf_op jit(solution)/shard_map/pallas_call | solution.py:149
  32.7 2.8 %broadcast_compare_fusion.1 = (pred[4]{0:T(512)(128)(4,1)S(1)}, s32[4]{0:T(128)S(1)}) fusion(s32[]{:T(128)S(6)} %add.7, s32[1]{0:T(128)} %bitcast.3, s32[1]{0:T(128)} %bitcast.2, s32[1]{0:T(128)} %bitcast.1, s32[1]{0:T(128)} %bitcast), kind=kLoop, calls=%fused_computation.3 | loop fusion | flops 16 | bytes 40 | tf_op jit(solution)/shard_map/eq | solution.py:335
  35.7 1.2 shard_map.70
  36.9 0.7 collective-permute-start.4
  37.6 2.5 %collective-permute-start.5 = (bf16[1024,128]{1,0:T(8,128)(2,1)S(1)}, bf16[1024,128]{1,0:T(8,128)(2,1)S(1)}, u32[]{:S(2)}, u32[]{:S(2)}) collective-permute-start(bf16[1024,128]{1,0:T(8,128)(2,1)S(1)} %get-tuple-element.30), channel_id=1, source_target_pairs={{1,2},{3,4},{5,6},{7,8},{9,10},{11,12},{13,14},{2,1},{4,3},{6,5},{... | collective-permute-start | bytes 786440 | tf_op jit(solution)/shard_map/ppermute | solution.py:321
  40.1 6.8 %collective-permute-start.6 = (bf16[1024,128]{1,0:T(8,128)(2,1)S(1)}, bf16[1024,128]{1,0:T(8,128)(2,1)S(1)}, u32[]{:S(2)}, u32[]{:S(2)}) collective-permute-start(bf16[1024,128]{1,0:T(8,128)(2,1)S(1)} %get-tuple-element.31), channel_id=1, source_target_pairs={{0,16},{16,0},{32,48},{48,32},{64,80},{80,64},{96,112},{112,96},{1... | collective-permute-start | bytes 786440 | tf_op jit(solution)/shard_map/ppermute | solution.py:322
  46.9 0.7 shard_map.69.own_ref
  47.7 2.9 %collective-permute-done.6.g2 = bf16[1024,128]{1,0:T(8,128)(2,1)S(1)} collective-permute-done((bf16[1024,128]{1,0:T(8,128)(2,1)S(1)}, bf16[1024,128]{1,0:T(8,128)(2,1)S(1)}, u32[]{:S(2)}, u32[]{:S(2)}) %collective-permute-start.6) | collective-permute-done | bytes 262176 | tf_op jit(solution)/shard_map/ppermute | solution.py:322
  50.7 3.1 %shard_map.71 = (f32[1024,128]{1,0:T(8,128)S(1)}, f32[1024,128]{1,0:T(8,128)S(1)}, bf16[1024,128]{1,0:T(8,128)(2,1)S(1)}, bf16[1024,128]{1,0:T(8,128)(2,1)S(1)},...) custom-call(s32[8]{0:T(128)S(1)} %add_convert_fusion.flags, f32[1024,128]{1,0:T(8,128)S(1)} %shard_map.69.own_ref, ...), custom_call_target="tpu_custom_call" | custom-call | tf_op jit(solution)/shard_map/pallas_call | solution.py:358
  53.7 0.7 collective-permute-start.8
  54.4 4.6 %collective-permute-start.9 = (bf16[1024,128]{1,0:T(8,128)(2,1)S(1)}, bf16[1024,128]{1,0:T(8,128)(2,1)S(1)}, u32[]{:S(2)}, u32[]{:S(2)}) collective-permute-start(bf16[1024,128]{1,0:T(8,128)(2,1)S(1)} %get-tuple-element.35), channel_id=1, source_target_pairs={{1,2},{3,4},{5,6},{7,8},{9,10},{11,12},{13,14},{2,1},{4,3},{6,5},{... | collective-permute-start | bytes 786440 | tf_op jit(solution)/shard_map/ppermute | solution.py:321
  59.0 5.4 %collective-permute-start.10 = (bf16[1024,128]{1,0:T(8,128)(2,1)S(1)}, bf16[1024,128]{1,0:T(8,128)(2,1)S(1)}, u32[]{:S(2)}, u32[]{:S(2)}) collective-permute-start(bf16[1024,128]{1,0:T(8,128)(2,1)S(1)} %get-tuple-element.36), channel_id=1, source_target_pairs={{0,16},{16,0},{32,48},{48,32},{64,80},{80,64},{96,112},{112,96},{1... | collective-permute-start | bytes 786440 | tf_op jit(solution)/shard_map/ppermute | solution.py:322
  64.4 0.7 shard_map.72.own_ref
  65.1 3.0 %collective-permute-done.10.g2 = bf16[1024,128]{1,0:T(8,128)(2,1)S(1)} collective-permute-done((bf16[1024,128]{1,0:T(8,128)(2,1)S(1)}, bf16[1024,128]{1,0:T(8,128)(2,1)S(1)}, u32[]{:S(2)}, u32[]{:S(2)}) %collective-permute-start.10) | collective-permute-done | bytes 262176 | tf_op jit(solution)/shard_map/ppermute | solution.py:322
  68.2 3.1 %shard_map.73 = (f32[1024,128]{1,0:T(8,128)S(1)}, f32[1024,128]{1,0:T(8,128)S(1)}, bf16[1024,128]{1,0:T(8,128)(2,1)S(1)}, bf16[1024,128]{1,0:T(8,128)(2,1)S(1)},...) custom-call(s32[8]{0:T(128)S(1)} %add_convert_fusion.flags, f32[1024,128]{1,0:T(8,128)S(1)} %shard_map.72.own_ref, ...), custom_call_target="tpu_custom_call" | custom-call | tf_op jit(solution)/shard_map/pallas_call | solution.py:358
  71.2 0.7 collective-permute-start.12
  71.9 2.9 %collective-permute-start.13 = (bf16[1024,128]{1,0:T(8,128)(2,1)S(1)}, bf16[1024,128]{1,0:T(8,128)(2,1)S(1)}, u32[]{:S(2)}, u32[]{:S(2)}) collective-permute-start(bf16[1024,128]{1,0:T(8,128)(2,1)S(1)} %get-tuple-element.43), channel_id=1, source_target_pairs={{1,2},{3,4},{5,6},{7,8},{9,10},{11,12},{13,14},{2,1},{4,3},{6,5},{... | collective-permute-start | bytes 786440 | tf_op jit(solution)/shard_map/ppermute | solution.py:321
  74.8 6.0 %collective-permute-start.14 = (bf16[1024,128]{1,0:T(8,128)(2,1)S(1)}, bf16[1024,128]{1,0:T(8,128)(2,1)S(1)}, u32[]{:S(2)}, u32[]{:S(2)}) collective-permute-start(bf16[1024,128]{1,0:T(8,128)(2,1)S(1)} %get-tuple-element.44), channel_id=1, source_target_pairs={{0,16},{16,0},{32,48},{48,32},{64,80},{80,64},{96,112},{112,96},{1... | collective-permute-start | bytes 786440 | tf_op jit(solution)/shard_map/ppermute | solution.py:322
  80.8 0.7 shard_map.74.own_ref
  81.6 3.0 %collective-permute-done.14.g2 = bf16[1024,128]{1,0:T(8,128)(2,1)S(1)} collective-permute-done((bf16[1024,128]{1,0:T(8,128)(2,1)S(1)}, bf16[1024,128]{1,0:T(8,128)(2,1)S(1)}, u32[]{:S(2)}, u32[]{:S(2)}) %collective-permute-start.14) | collective-permute-done | bytes 262176 | tf_op jit(solution)/shard_map/ppermute | solution.py:322
  84.6 3.0 %shard_map.75 = f32[16,16,128]{2,1,0:T(8,128)S(1)} custom-call(s32[8]{0:T(128)S(1)} %add_convert_fusion.flags, f32[1024,128]{1,0:T(8,128)S(1)} %shard_map.74.own_ref, bf16[1024,1024]{1,0:T(8,128)(2,1)S(1)} %bitcast.16, bf16[1024,1024]{1,0:T(8,128)(2,1)S(1)} %get-tuple-element.27.high_ref, bf16[1024,1024]{1,0:T(8,128)(2,1)S(1)} %get-tuple-element.28.low_ref, ...), custom_call_target="tpu_custom_call" | custom-call | tf_op jit(solution)/shard_map/pallas_call | solution.py:369
  87.6 17.3 %all_to_all.10.in_ref = f32[16,16,128]{2,1,0:T(8,128)} all-to-all(f32[16,16,128]{2,1,0:T(8,128)S(1)} %shard_map.75), channel_id=1, replica_groups=mesh['tr'=16,'tc'=16] {'tc'}, dimensions={0} | all-to-all | bytes 262144 | tf_op jit(solution)/shard_map/all_to_all | solution.py:377
  104.9 1.7 %shard_map.76 = f32[16,16,128]{2,1,0:T(8,128)} custom-call(f32[16,16,128]{2,1,0:T(8,128)} %all_to_all.10.in_ref), custom_call_target="tpu_custom_call" | custom-call | tf_op jit(solution)/shard_map/pallas_call | solution.py:378
  106.6 19.2 %all_to_all.11.in_ref = f32[16,16,128]{2,1,0:T(8,128)S(1)} all-to-all(f32[16,16,128]{2,1,0:T(8,128)} %shard_map.76), channel_id=1, replica_groups=mesh['tr'=16,'tc'=16] {'tr'}, dimensions={0} | all-to-all | bytes 262144 | tf_op jit(solution)/shard_map/all_to_all | solution.py:384
  125.7 1.1 shard_map.77
  (23 shorter events, 0.2 us)
Async XLA Ops:
  1.3 31.4 %collective-permute-start.3 = (s32[1,1]{1,0:T(1,128)}, s32[1,1]{1,0:T(1,128)}, u32[]{:S(2)}, u32[]{:S(2)}) collective-permute-start(s32[1,1]{1,0:T(1,128)} %add.6), channel_id=1, source_target_pairs={{0,1},{1,0},{2,3},{3,2},{4,5},{5,4},{6,7},{7,6},{8,9},{9,8},{10,11... | collective-permute-start | bytes 20 | tf_op jit(solution)/shard_map/ppermute | solution.py:323
  5.4 27.3 %collective-permute-start.2 = (s32[1,1]{1,0:T(1,128)}, s32[1,1]{1,0:T(1,128)}, u32[]{:S(2)}, u32[]{:S(2)}) collective-permute-start(s32[1,1]{1,0:T(1,128)} %add.6), channel_id=1, source_target_pairs={{0,16},{16,0},{32,48},{48,32},{64,80},{80,64},{96,112},{112,96},{1... | collective-permute-start | bytes 20 | tf_op jit(solution)/shard_map/ppermute | solution.py:322
  6.2 26.6 %collective-permute-start.1 = (s32[1,1]{1,0:T(1,128)}, s32[1,1]{1,0:T(1,128)}, u32[]{:S(2)}, u32[]{:S(2)}) collective-permute-start(s32[1,1]{1,0:T(1,128)} %add.6), channel_id=1, source_target_pairs={{1,2},{3,4},{5,6},{7,8},{9,10},{11,12},{13,14},{2,1},{4,3},{6,5},{... | collective-permute-start | bytes 20 | tf_op jit(solution)/shard_map/ppermute | solution.py:321
  10.6 22.1 %collective-permute-start = (s32[1,1]{1,0:T(1,128)}, s32[1,1]{1,0:T(1,128)}, u32[]{:S(2)}, u32[]{:S(2)}) collective-permute-start(s32[1,1]{1,0:T(1,128)} %add.6), channel_id=1, source_target_pairs={{16,32},{48,64},{80,96},{112,128},{144,160},{176,192},{208,224},{3... | collective-permute-start | bytes 20 | tf_op jit(solution)/shard_map/ppermute | solution.py:320
  11.9 1.6 %copy-start = (bf16[1,1,1024,1024]{3,2,1,0:T(8,128)(2,1)S(1)}, bf16[1,1,1024,1024]{3,2,1,0:T(8,128)(2,1)}, u32[]{:S(2)}) copy-start(bf16[1,1,1024,1024]{3,2,1,0:T(8,128)(2,1)} %param.6) | copy-start | bytes 6291460
  13.4 2.2 %copy-start.2 = (f32[1,1,1024,1024]{3,2,1,0:T(8,128)S(1)}, f32[1,1,1024,1024]{3,2,1,0:T(8,128)}, u32[]{:S(2)}) copy-start(f32[1,1,1024,1024]{3,2,1,0:T(8,128)} %param.7) | copy-start | bytes 12582916
  15.6 1.0 copy-start.3
  32.7 14.2 %copy-start.1 = (bf16[1,1,1024,1024]{3,2,1,0:T(8,128)(2,1)S(1)}, bf16[1,1,1024,1024]{3,2,1,0:T(8,128)(2,1)}, u32[]{:S(2)}) copy-start(bf16[1,1,1024,1024]{3,2,1,0:T(8,128)(2,1)} %param.5) | copy-start | bytes 6291460
  36.9 10.7 %collective-permute-start.4 = (bf16[1024,128]{1,0:T(8,128)(2,1)S(1)}, bf16[1024,128]{1,0:T(8,128)(2,1)S(1)}, u32[]{:S(2)}, u32[]{:S(2)}) collective-permute-start(bf16[1024,128]{1,0:T(8,128)(2,1)S(1)} %get-tuple-element.29), channel_id=1, source_target_pairs={{16,32},{48,64},{80,96},{112,128},{144,160},{176,192},{208,224},{3... | collective-permute-start | bytes 786440 | tf_op jit(solution)/shard_map/ppermute | solution.py:320
  37.6 10.1 %collective-permute-start.5 = (bf16[1024,128]{1,0:T(8,128)(2,1)S(1)}, bf16[1024,128]{1,0:T(8,128)(2,1)S(1)}, u32[]{:S(2)}, u32[]{:S(2)}) collective-permute-start(bf16[1024,128]{1,0:T(8,128)(2,1)S(1)} %get-tuple-element.30), channel_id=1, source_target_pairs={{1,2},{3,4},{5,6},{7,8},{9,10},{11,12},{13,14},{2,1},{4,3},{6,5},{... | collective-permute-start | bytes 786440 | tf_op jit(solution)/shard_map/ppermute | solution.py:321
  40.1 10.6 %collective-permute-start.6 = (bf16[1024,128]{1,0:T(8,128)(2,1)S(1)}, bf16[1024,128]{1,0:T(8,128)(2,1)S(1)}, u32[]{:S(2)}, u32[]{:S(2)}) collective-permute-start(bf16[1024,128]{1,0:T(8,128)(2,1)S(1)} %get-tuple-element.31), channel_id=1, source_target_pairs={{0,16},{16,0},{32,48},{48,32},{64,80},{80,64},{96,112},{112,96},{1... | collective-permute-start | bytes 786440 | tf_op jit(solution)/shard_map/ppermute | solution.py:322
  46.9 3.8 %collective-permute-start.7 = (bf16[1024,128]{1,0:T(8,128)(2,1)S(1)}, bf16[1024,128]{1,0:T(8,128)(2,1)S(1)}, u32[]{:S(2)}, u32[]{:S(2)}) collective-permute-start(bf16[1024,128]{1,0:T(8,128)(2,1)S(1)} %get-tuple-element.32), channel_id=1, source_target_pairs={{0,1},{1,0},{2,3},{3,2},{4,5},{5,4},{6,7},{7,6},{8,9},{9,8},{10,11... | collective-permute-start | bytes 786440 | tf_op jit(solution)/shard_map/ppermute | solution.py:323
  53.7 11.4 %collective-permute-start.8 = (bf16[1024,128]{1,0:T(8,128)(2,1)S(1)}, bf16[1024,128]{1,0:T(8,128)(2,1)S(1)}, u32[]{:S(2)}, u32[]{:S(2)}) collective-permute-start(bf16[1024,128]{1,0:T(8,128)(2,1)S(1)} %get-tuple-element.34), channel_id=1, source_target_pairs={{16,32},{48,64},{80,96},{112,128},{144,160},{176,192},{208,224},{3... | collective-permute-start | bytes 786440 | tf_op jit(solution)/shard_map/ppermute | solution.py:320
  54.4 10.7 %collective-permute-start.9 = (bf16[1024,128]{1,0:T(8,128)(2,1)S(1)}, bf16[1024,128]{1,0:T(8,128)(2,1)S(1)}, u32[]{:S(2)}, u32[]{:S(2)}) collective-permute-start(bf16[1024,128]{1,0:T(8,128)(2,1)S(1)} %get-tuple-element.35), channel_id=1, source_target_pairs={{1,2},{3,4},{5,6},{7,8},{9,10},{11,12},{13,14},{2,1},{4,3},{6,5},{... | collective-permute-start | bytes 786440 | tf_op jit(solution)/shard_map/ppermute | solution.py:321
  59.0 9.2 %collective-permute-start.10 = (bf16[1024,128]{1,0:T(8,128)(2,1)S(1)}, bf16[1024,128]{1,0:T(8,128)(2,1)S(1)}, u32[]{:S(2)}, u32[]{:S(2)}) collective-permute-start(bf16[1024,128]{1,0:T(8,128)(2,1)S(1)} %get-tuple-element.36), channel_id=1, source_target_pairs={{0,16},{16,0},{32,48},{48,32},{64,80},{80,64},{96,112},{112,96},{1... | collective-permute-start | bytes 786440 | tf_op jit(solution)/shard_map/ppermute | solution.py:322
  64.4 3.8 %collective-permute-start.11 = (bf16[1024,128]{1,0:T(8,128)(2,1)S(1)}, bf16[1024,128]{1,0:T(8,128)(2,1)S(1)}, u32[]{:S(2)}, u32[]{:S(2)}) collective-permute-start(bf16[1024,128]{1,0:T(8,128)(2,1)S(1)} %get-tuple-element.37), channel_id=1, source_target_pairs={{0,1},{1,0},{2,3},{3,2},{4,5},{5,4},{6,7},{7,6},{8,9},{9,8},{10,11... | collective-permute-start | bytes 786440 | tf_op jit(solution)/shard_map/ppermute | solution.py:323
  71.2 10.3 %collective-permute-start.12 = (bf16[1024,128]{1,0:T(8,128)(2,1)S(1)}, bf16[1024,128]{1,0:T(8,128)(2,1)S(1)}, u32[]{:S(2)}, u32[]{:S(2)}) collective-permute-start(bf16[1024,128]{1,0:T(8,128)(2,1)S(1)} %get-tuple-element.42), channel_id=1, source_target_pairs={{16,32},{48,64},{80,96},{112,128},{144,160},{176,192},{208,224},{3... | collective-permute-start | bytes 786440 | tf_op jit(solution)/shard_map/ppermute | solution.py:320
  71.9 9.7 %collective-permute-start.13 = (bf16[1024,128]{1,0:T(8,128)(2,1)S(1)}, bf16[1024,128]{1,0:T(8,128)(2,1)S(1)}, u32[]{:S(2)}, u32[]{:S(2)}) collective-permute-start(bf16[1024,128]{1,0:T(8,128)(2,1)S(1)} %get-tuple-element.43), channel_id=1, source_target_pairs={{1,2},{3,4},{5,6},{7,8},{9,10},{11,12},{13,14},{2,1},{4,3},{6,5},{... | collective-permute-start | bytes 786440 | tf_op jit(solution)/shard_map/ppermute | solution.py:321
  74.8 9.8 %collective-permute-start.14 = (bf16[1024,128]{1,0:T(8,128)(2,1)S(1)}, bf16[1024,128]{1,0:T(8,128)(2,1)S(1)}, u32[]{:S(2)}, u32[]{:S(2)}) collective-permute-start(bf16[1024,128]{1,0:T(8,128)(2,1)S(1)} %get-tuple-element.44), channel_id=1, source_target_pairs={{0,16},{16,0},{32,48},{48,32},{64,80},{80,64},{96,112},{112,96},{1... | collective-permute-start | bytes 786440 | tf_op jit(solution)/shard_map/ppermute | solution.py:322
  80.8 3.8 %collective-permute-start.15 = (bf16[1024,128]{1,0:T(8,128)(2,1)S(1)}, bf16[1024,128]{1,0:T(8,128)(2,1)S(1)}, u32[]{:S(2)}, u32[]{:S(2)}) collective-permute-start(bf16[1024,128]{1,0:T(8,128)(2,1)S(1)} %get-tuple-element.45), channel_id=1, source_target_pairs={{0,1},{1,0},{2,3},{3,2},{4,5},{5,4},{6,7},{7,6},{8,9},{9,8},{10,11... | collective-permute-start | bytes 786440 | tf_op jit(solution)/shard_map/ppermute | solution.py:323
